TPU v7x, 1024 devices: a whole 4x8x16 slice. The times are simulated.
1024 devices in a mesh: shot: 32 (over y, x_hi, core), slab: 32 (over z, x_lo).
Axes of the slice: x: 4 (x_hi: 2, x_lo: 2; x = x_hi * 2 + x_lo), y: 8, z: 16, core: 2. Of those that a mesh axis runs over, the one named last changes fastest.
Arguments:
- courant: float32 [128, 32, 128], P('slab'), may hold values from 0.04 to 0.16
- buoyancy: float32 [128, 32, 128], P('slab'), may hold values from 0.5 to 2
- wave_before: float32 [32, 128, 32, 128], P('shot', 'slab'), may hold values from -6 to 6
- wave_now: float32 [32, 128, 32, 128], P('shot', 'slab'), may hold values from -6 to 6
- wavelet: float32 [32, 6], P('shot'), may hold values from -16 to 16
- source_cell: int32 [32, 1], P('shot'), may hold values from 0 to 524287
- observed: float32 [32, 6, 16384], P('shot', None, 'slab'), may hold values from -6 to 6
- receiver_slab: int32 [32, 16384, 1], P('shot', 'slab'), may hold values from 0 to 31; in each aligned block of 512 rows (0 to 511, 512 to 1023, ..., all dimensions but the last counted through in order) at most 32 rows name the same one
- receiver_cell: int32 [32, 16384], P('shot', 'slab'), may hold values from 0 to 16383
Outputs:
- grad_courant: float32 [128, 32, 128], P('slab')
- grad_buoyancy: float32 [128, 32, 128], P('slab')
Inputs may be any that keep to these rules, and one draw needn't show every extreme that they name: `receiver_slab`: among the receivers held by one device no slab is named more than 32 times; for some devices one slab is named exactly 32 times.
All inputs are finite; a program needn't handle non-finite values.
Results may differ from a plain program's by a relative error of at most 0.0003.
Values sent between devices are 32-bit elements; how exact they have to be, the bound alone decides.
No kernel may reach another device: no remote copies, remote signals or barrier semaphores. Data moves between devices by JAX's collectives and lax.ppermute only.
A program may use at most 32 MiB of HBM per device.

v0:
```python
import jax
import jax.numpy as jnp
from jax import lax
from jax.experimental import pallas as pl
from jax.experimental.pallas import tpu as pltpu
from jax.sharding import PartitionSpec as P

STEPS = 6
NZ = 32
NY = 128
ROWS = 4
PLANE = NZ * NY
PLANE_BITS = 12
SLABS = 32
SHOTS = 32
CAP = 32
REACH = 3
EXT = ROWS * (2 * REACH + 1)
OWN = ROWS * REACH
LO = 4
BAND = 20
SHIFTS = (1, -1, 2, -2, 3, -3)

NT = (((1,), (1,)), ((), ()))


def split_bf16(x, pieces):
    out = []
    for _ in range(pieces):
        part = x.astype(jnp.bfloat16)
        out.append(part)
        x = x - part.astype(jnp.float32)
    return out


def iota(shape, axis):
    return lax.broadcasted_iota(jnp.int32, shape, axis)


def mxu(a, b, dims):
    return lax.dot_general(a, b, dims, preferred_element_type=jnp.float32)


def route_kernel(slab_ref, cell_ref, obs_ref, out_ref):
    rec = slab_ref.shape[1]
    slab = slab_ref[...]
    hot = (iota((SLABS, rec), 0) == slab).astype(jnp.float32)
    hot16 = hot.astype(jnp.bfloat16)
    tri = (iota((rec, rec), 0) < iota((rec, rec), 1)).astype(jnp.float32).astype(jnp.bfloat16)
    earlier = mxu(hot16, tri, (((1,), (0,)), ((), ())))
    rank = jnp.sum(earlier * hot, axis=0, keepdims=True).astype(jnp.int32)
    at_slot = iota((CAP, rec), 0) == rank
    cells = (cell_ref[...] + 1).astype(jnp.float32)
    values = [obs_ref[n] for n in range(STEPS)] + [cells]
    total = None
    splits = [split_bf16(v, 3) for v in values]
    for p in range(3):
        rows = [jnp.where(at_slot, s[p].astype(jnp.float32), 0.0) for s in splits]
        rows.append(jnp.zeros((CAP, rec), jnp.float32))
        block = jnp.concatenate(rows, axis=0).astype(jnp.bfloat16)
        term = mxu(hot16, block, NT)
        total = term if total is None else total + term
    row = iota((SLABS, 128), 0)
    lane = iota((SLABS, 128), 1)

    def shifted(tile, shift):
        moved = pltpu.roll(tile, (-shift) % SLABS, 0)
        there = row + shift
        return jnp.where((there >= 0) & (there < SLABS), moved, 0.0)

    tiles = [total[:, 128 * t : 128 * t + 128] for t in range(2)]
    by_shift = {s: [shifted(t, s) if s else t for t in tiles] for s in (-2, -1, 0, 1, 2)}

    def piece(shift, value, group):
        tile = by_shift[shift][value // 4]
        return pltpu.roll(tile, (CAP * (group - value % 4)) % 128, 1) if (group - value % 4) % 4 else tile

    for v in range(8):
        if v < 7:
            near = jnp.where(lane < CAP, piece(-1, v, 0), jnp.where(lane < 2 * CAP, piece(0, v, 1), piece(1, v, 2)))
        else:
            near = jnp.zeros((SLABS, 128), jnp.float32)
        if v < 3:
            far = piece(-2, v + 4, 3)
        elif v < 6:
            far = piece(2, v + 1, 3)
        else:
            far = jnp.zeros((SLABS, 128), jnp.float32)
        out_ref[:, v, :] = jnp.where(lane < 3 * CAP, near, far)


def scatter_dense(cell_row, value_rows, halves):
    count = cell_row.shape[1]
    cell = cell_row.astype(jnp.int32) - 1
    half = lax.shift_right_arithmetic(cell, 13)
    lane_of = cell & 127
    if halves is None:
        spot, width = half * 128 + lane_of, 256
    else:
        spot, width = jnp.where(half == halves, lane_of, -1), 128
    right = (iota((width, count), 0) == spot).astype(jnp.float32).astype(jnp.bfloat16)
    left_hot = iota((64, count), 0) == (lax.shift_right_arithmetic(cell, 7) & 63)
    zero = jnp.zeros((64, count), jnp.float32)
    splits = [split_bf16(v, 2) for v in value_rows]
    blocks = [jnp.where(left_hot, 1.0, zero).astype(jnp.bfloat16)]
    lows = []
    for s in splits:
        blocks.append(jnp.where(left_hot, s[0].astype(jnp.float32), zero).astype(jnp.bfloat16))
        lows.append(jnp.where(left_hot, s[1].astype(jnp.float32), zero).astype(jnp.bfloat16))
    main = mxu(jnp.concatenate(blocks, axis=0), right, NT)
    rest = mxu(jnp.concatenate(lows, axis=0), right, NT)
    out = [main[0:64]]
    for i in range(len(splits)):
        out.append(main[64 * (i + 1) : 64 * (i + 2)] + rest[64 * i : 64 * (i + 1)])
    return out


def scatter_kernel(wavelet_ref, got_ref, count, traces, pulses):
    for n in range(8):
        pulses[n : n + 1] = jnp.full((1, NY), wavelet_ref[0, n] if n < STEPS else 0.0)
    lane8 = iota((8, 128), 1)
    blocks = [[], [], [], []]
    for j in range(SLABS // 4):
        quad = [got_ref[4 * j + i] for i in range(4)]
        for q in range(4):
            merged = None
            for i in range(4):
                turn = (CAP * (i - q)) % 128
                moved = pltpu.roll(quad[i], turn, 1) if turn else quad[i]
                merged = moved if merged is None else jnp.where(lane8 >= CAP * i, moved, merged)
            blocks[q].append(merged)
    lists = [jnp.concatenate(b, axis=1) for b in blocks]
    for q in range(3):
        rows = lists[q]
        parts = scatter_dense(rows[6:7], [rows[n : n + 1] for n in range(STEPS)], None)
        base = OWN + ROWS * (q - 1) - LO
        for i, part in enumerate(parts):
            for a in range(ROWS):
                value = part[NZ * (a % 2) : NZ * (a % 2) + NZ, 128 * (a // 2) : 128 * (a // 2) + 128]
                if i == 0:
                    count[base + a] = value
                else:
                    traces[i - 1, base + a] = value
    for side in range(2):
        rows = lists[3][3 * side : 3 * side + 3]
        parts = scatter_dense(rows[2:3], [rows[0:1], rows[1:2]], 1 - side)
        base = (OWN - 2 * ROWS + 2 if side == 0 else OWN + 2 * ROWS) - LO
        for i, part in enumerate(parts):
            for a in range(2):
                value = part[NZ * a : NZ * a + NZ]
                if i == 0:
                    count[base + a] = value
                else:
                    traces[STEPS - 3 + i, base + a] = value


def up_y(x):
    return pltpu.roll(x, NY - 1, 1)


def down_y(x):
    return pltpu.roll(x, 1, 1)


DEEP = NZ + 16
HERE = pl.ds(8, NZ)
UP = pl.ds(9, NZ)
DOWN = pl.ds(7, NZ)


def operate(faces, field, rows, base, lo, hi, emit):
    cx, czp, czm, cyp, cym, diag = faces
    before, here = field[(*rows, lo - 1 - base, HERE)], field[(*rows, lo - base, HERE)]
    for r in range(lo, hi):
        after = field[(*rows, r + 1 - base, HERE)]
        total = cx[r] * after + cx[r - 1] * before
        total += czp[r] * field[(*rows, r - base, UP)] + czm[r] * field[(*rows, r - base, DOWN)]
        total += cyp[r] * up_y(here) + cym[r] * down_y(here)
        emit(r, here, total - diag[r] * here)
        before, here = here, after


def window_kernel(source_ref, mine_ref, *refs):
    near_refs = refs[: 2 * REACH]
    count, traces, pulses, out_ref, lap, ext, wave, cx, czp, czm, cyp, cym, diag, adj, weighted = refs[2 * REACH :]
    slab = lax.axis_index("slab")

    for f in range(2):
        ext[f, OWN : OWN + ROWS] = mine_ref[f]
        wave[f, OWN : OWN + ROWS, HERE] = mine_ref[f + 2]
    for i, ref in enumerate(near_refs):
        start = OWN - ROWS * SHIFTS[i]
        for f in range(2):
            ext[f, start : start + ROWS] = ref[f]
            wave[f, start : start + ROWS, HERE] = ref[f + 2]

    zpos = iota((NZ, NY), 0)
    ypos = iota((NZ, NY), 1)
    z_last, z_first, y_last = zpos == NZ - 1, zpos == 0, ypos == NY - 1
    y_end = 0.5 * (y_last | (ypos == 0)).astype(jnp.float32)
    pad = jnp.zeros((8, NY), jnp.float32)
    for r in range(EXT):
        for n in range(STEPS + 2):
            wave[n, r, 0:8] = pad
            wave[n, r, NZ + 8 : DEEP] = pad
    for r in range(BAND):
        for n in range(3):
            weighted[n, r, 0:8] = pad
            weighted[n, r, NZ + 8 : DEEP] = pad
    for r in range(EXT):
        b = ext[1, r]
        if r + 1 < EXT:
            cx[r] = 0.5 * (b + ext[1, r + 1])
        if 0 < r < EXT - 1:
            up = 0.5 * (b + jnp.where(z_last, 0.0, pltpu.roll(b, NZ - 1, 0)))
            down = 0.5 * (b + jnp.where(z_first, 0.0, pltpu.roll(b, 1, 0)))
            right = jnp.where(y_last, 0.0, 0.5 * (b + up_y(b)))
            left = down_y(right)
            czp[r], czm[r], cyp[r], cym[r] = up, down, right, left
            diag[r] = (cx[r - 1] + cx[r]) + (up + down) + (right + left + y_end * b)

    faces = (cx, czp, czm, cyp, cym, diag)
    local_source = source_ref[0, 0] - (slab * ROWS - OWN) * PLANE
    source_row = jnp.clip(lax.shift_right_arithmetic(local_source, PLANE_BITS), 0, EXT - 1)
    at_source = zpos * NY + ypos == local_source - source_row * PLANE

    def step(n, carry):
        pulse = pulses[pl.ds(n, 1)]

        def emit(r, here, total):
            if OWN <= r < OWN + ROWS:
                lap[n, r - OWN] = total
            wave[n + 2, r, HERE] = (here + here) - wave[n, r, HERE] + ext[0, r] * total

        operate(faces, wave, (n + 1,), 0, 1, EXT - 1, emit)
        wave[n + 2, source_row, HERE] = wave[n + 2, source_row, HERE] + jnp.where(at_source, pulse, 0.0)
        return carry

    lax.fori_loop(0, STEPS, step, 0)

    grad_q = [None] * ROWS
    px = [None] * (ROWS + 1)
    pz = [None] * ROWS
    py = [None] * ROWS
    both = [None] * ROWS

    def add(total, term):
        return term if total is None else total + term

    for k in range(STEPS, 0, -1):
        slot, after, older = k % 3, (k + 1) % 3, (k + 2) % 3

        def residual(r, k=k):
            return count[r - LO] * wave[k + 1, r, HERE] - traces[k - 1, r - LO]

        def store(r, value, slot=slot):
            adj[slot, r - LO] = value
            weighted[slot, r - LO, HERE] = ext[0, r] * value

        if k == STEPS:
            for r in range(OWN - k, OWN + ROWS + k):
                store(r, residual(r))
        else:

            def emit_adj(r, here, total, k=k, after=after, older=older, residual=residual, store=store):
                value = residual(r) + 2.0 * adj[after, r - LO] + total
                if k < STEPS - 1:
                    value = value - adj[older, r - LO]
                store(r, value)

            operate(faces, weighted, (after,), LO, OWN - k, OWN + ROWS + k, emit_adj)

        for a in range(ROWS + 1):
            r = OWN + a
            u, w = wave[k, r, HERE], weighted[slot, r - LO, HERE]
            du = u - wave[k, r - 1, HERE]
            dw = w - weighted[slot, r - 1 - LO, HERE]
            px[a] = add(px[a], du * dw)
            if a < ROWS:
                grad_q[a] = add(grad_q[a], adj[slot, r - LO] * lap[k - 1, a])
                both[a] = add(both[a], u * w)
                pz[a] = add(pz[a], (wave[k, r, UP] - u) * (weighted[slot, r - LO, UP] - w))
                py[a] = add(py[a], (up_y(u) - u) * (up_y(w) - w))

    for a in range(ROWS):
        z_up = pz[a]
        z_down = jnp.where(z_first, both[a], pltpu.roll(pz[a], 1, 0))
        y_up = jnp.where(y_last, both[a], py[a])
        y_down = jnp.where(ypos == 0, both[a], down_y(py[a]))
        grad_b = -0.5 * (((px[a] + px[a + 1]) + (z_up + z_down)) + (y_up + y_down))
        out_ref[a] = grad_q[a]
        out_ref[ROWS + a] = grad_b


def vmem(shape):
    return pltpu.VMEM(shape, jnp.float32)


def shift_pairs(shift):
    return [(i, i + shift) for i in range(SLABS) if 0 <= i + shift < SLABS]


def local(
    courant,
    buoyancy,
    wave_before,
    wave_now,
    wavelet,
    source_cell,
    observed,
    receiver_slab,
    receiver_cell,
):
    rec = receiver_cell.shape[1]
    mine = jnp.stack([courant, buoyancy, wave_before[0], wave_now[0]])
    near = [lax.ppermute(mine, "slab", shift_pairs(shift)) for shift in SHIFTS]
    send = pl.pallas_call(
        route_kernel,
        out_shape=jax.ShapeDtypeStruct((SLABS, 8, 128), jnp.float32),
        name="route",
    )(receiver_slab.reshape(1, rec), receiver_cell, observed.transpose(1, 0, 2))
    got = lax.all_to_all(send, "slab", 0, 0, tiled=True)
    smem = pl.BlockSpec(memory_space=pltpu.SMEM)
    whole = pl.BlockSpec(memory_space=pltpu.VMEM)
    count, traces, pulses = pl.pallas_call(
        scatter_kernel,
        out_shape=(
            jax.ShapeDtypeStruct((BAND, NZ, NY), jnp.float32),
            jax.ShapeDtypeStruct((STEPS, BAND, NZ, NY), jnp.float32),
            jax.ShapeDtypeStruct((8, NY), jnp.float32),
        ),
        in_specs=[smem, whole],
        out_specs=(whole, whole, whole),
        compiler_params=pltpu.CompilerParams(vmem_limit_bytes=24 * 2**20),
        name="scatter",
    )(wavelet, got)
    grads = pl.pallas_call(
        window_kernel,
        out_shape=jax.ShapeDtypeStruct((2 * ROWS, NZ, NY), jnp.float32),
        in_specs=[smem] + [whole] * (2 * REACH + 4),
        out_specs=whole,
        scratch_shapes=[
            vmem((STEPS, ROWS, NZ, NY)),
            vmem((2, EXT, NZ, NY)),
            vmem((STEPS + 2, EXT, DEEP, NY)),
            vmem((EXT, NZ, NY)),
            vmem((EXT, NZ, NY)),
            vmem((EXT, NZ, NY)),
            vmem((EXT, NZ, NY)),
            vmem((EXT, NZ, NY)),
            vmem((EXT, NZ, NY)),
            vmem((3, BAND, NZ, NY)),
            vmem((3, BAND, DEEP, NY)),
        ],
        compiler_params=pltpu.CompilerParams(vmem_limit_bytes=24 * 2**20),
        name="window",
    )(source_cell, mine, *near, count, traces, pulses)
    terms = lax.all_to_all(grads.reshape(SHOTS, 8, NY), "shot", 0, 0, tiled=True)
    total = jnp.broadcast_to(jnp.sum(terms, axis=0), (SHOTS, 8, NY))
    full = lax.all_to_all(total, "shot", 0, 0, tiled=True).reshape(2, ROWS, NZ, NY)
    return full[0], full[1]


def solution(mesh):
    in_specs = (
        P("slab", None, None),
        P("slab", None, None),
        P("shot", "slab", None, None),
        P("shot", "slab", None, None),
        P("shot", None),
        P("shot", None),
        P("shot", None, "slab"),
        P("shot", "slab", None),
        P("shot", "slab"),
    )
    out_specs = (P("slab", None, None), P("slab", None, None))
    return jax.shard_map(local, mesh=mesh, in_specs=in_specs, out_specs=out_specs, check_vma=False)
```

profile of v0, /device:TPU:3, one launch (start us, length us, event | category | flops | bytes accessed | tf_op | source)
XLA Modules:
  0.0 97.9 jit_solution(13459291119909378745)
XLA Ops:
  0.6 1.0 pad_maximum_fusion.mine_ref
  1.6 4.0 %collective-permute-start = (f32[4,4,32,128]{3,2,1,0:T(8,128)S(1)}, f32[4,4,32,128]{3,2,1,0:T(8,128)S(1)}, u32[]{:S(2)}, u32[]{:S(2)}) collective-permute-start(f32[4,4,32,128]{3,2,1,0:T(8,128)S(1)} %pad_maximum_fusion.mine_ref), channel_id=1, source_target_pairs={{0,1},{1,2},{2,3},{3,4},{4,5},{5,6},{6,7},{7,8},{8,9},{9,10},{10,1... | collective-permute-start | bytes 786440 | tf_op jit(solution)/shard_map/ppermute | solution.py:316
  5.6 2.1 %route.1 = f32[32,8,128]{2,1,0:T(8,128)} custom-call(s32[1,512]{1,0:T(1,128)} %bitcast.13, s32[1,512]{1,0:T(1,128)} %cell_ref.1, f32[6,1,512]{2,1,0:T(1,128)} %bitcast.12), custom_call_target="tpu_custom_call" | custom-call | tf_op jit(solution)/shard_map/route/pallas_call | solution.py:317
  7.7 18.9 %all-to-all-start = ((f32[32,8,128]{2,1,0:T(8,128)}), f32[32,8,128]{2,1,0:T(8,128)S(1)}, u32[]{:S(2)}, u32[]{:S(2)}) async-start(f32[32,8,128]{2,1,0:T(8,128)} %route.1), calls=%async_computation | async-start | bytes 262144 | tf_op jit(solution)/shard_map/all_to_all | solution.py:322
  26.6 2.1 %collective-permute-start.1 = (f32[4,4,32,128]{3,2,1,0:T(8,128)S(1)}, f32[4,4,32,128]{3,2,1,0:T(8,128)S(1)}, u32[]{:S(2)}, u32[]{:S(2)}) collective-permute-start(f32[4,4,32,128]{3,2,1,0:T(8,128)S(1)} %pad_maximum_fusion.mine_ref), channel_id=1, source_target_pairs={{1,0},{2,1},{3,2},{4,3},{5,4},{6,5},{7,6},{8,7},{9,8},{10,9},{11,1... | collective-permute-start | bytes 786440 | tf_op jit(solution)/shard_map/ppermute | solution.py:316
  28.8 3.1 %collective-permute-start.2 = (f32[4,4,32,128]{3,2,1,0:T(8,128)S(1)}, f32[4,4,32,128]{3,2,1,0:T(8,128)S(1)}, u32[]{:S(2)}, u32[]{:S(2)}) collective-permute-start(f32[4,4,32,128]{3,2,1,0:T(8,128)S(1)} %pad_maximum_fusion.mine_ref), channel_id=1, source_target_pairs={{0,2},{1,3},{2,4},{3,5},{4,6},{5,7},{6,8},{7,9},{8,10},{9,11},{10,... | collective-permute-start | bytes 786440 | tf_op jit(solution)/shard_map/ppermute | solution.py:316
  31.9 1.3 %collective-permute-start.3 = (f32[4,4,32,128]{3,2,1,0:T(8,128)S(1)}, f32[4,4,32,128]{3,2,1,0:T(8,128)S(1)}, u32[]{:S(2)}, u32[]{:S(2)}) collective-permute-start(f32[4,4,32,128]{3,2,1,0:T(8,128)S(1)} %pad_maximum_fusion.mine_ref), channel_id=1, source_target_pairs={{2,0},{3,1},{4,2},{5,3},{6,4},{7,5},{8,6},{9,7},{10,8},{11,9},{12,... | collective-permute-start | bytes 786440 | tf_op jit(solution)/shard_map/ppermute | solution.py:316
  33.2 5.8 %collective-permute-start.4 = (f32[4,4,32,128]{3,2,1,0:T(8,128)S(1)}, f32[4,4,32,128]{3,2,1,0:T(8,128)S(1)}, u32[]{:S(2)}, u32[]{:S(2)}) collective-permute-start(f32[4,4,32,128]{3,2,1,0:T(8,128)S(1)} %pad_maximum_fusion.mine_ref), channel_id=1, source_target_pairs={{0,3},{1,4},{2,5},{3,6},{4,7},{5,8},{6,9},{7,10},{8,11},{9,12},{10... | collective-permute-start | bytes 786440 | tf_op jit(solution)/shard_map/ppermute | solution.py:316
  39.0 0.0 collective-permute-done.refs_0_
  39.0 1.3 %collective-permute-start.5 = (f32[4,4,32,128]{3,2,1,0:T(8,128)S(1)}, f32[4,4,32,128]{3,2,1,0:T(8,128)S(1)}, u32[]{:S(2)}, u32[]{:S(2)}) collective-permute-start(f32[4,4,32,128]{3,2,1,0:T(8,128)S(1)} %pad_maximum_fusion.mine_ref), channel_id=1, source_target_pairs={{3,0},{4,1},{5,2},{6,3},{7,4},{8,5},{9,6},{10,7},{11,8},{12,9},{13... | collective-permute-start | bytes 786440 | tf_op jit(solution)/shard_map/ppermute | solution.py:316
  41.0 0.2 all-to-all-done.got_ref
  41.2 0.0 copy-start
  41.2 0.7 copy-done
  41.8 2.5 %scatter.1 = (f32[20,32,128]{2,1,0:T(8,128)S(1)}, f32[6,20,32,128]{3,2,1,0:T(8,128)S(1)}, f32[8,128]{1,0:T(8,128)S(1)}) custom-call(f32[1,6]{1,0:T(1,128)S(1)} %copy-done, f32[32,8,128]{2,1,0:T(8,128)S(1)} %all-to-all-done.got_ref), custom_call_target="tpu_custom_call" | custom-call | tf_op jit(solution)/shard_map/scatter/pallas_call | solution.py:325
  44.3 0.0 collective-permute-done.1.refs_1_
  44.4 0.0 collective-permute-done.2.refs_2_
  44.4 0.0 collective-permute-done.3.refs_3_
  44.4 0.0 collective-permute-done.4.refs_4_
  44.4 13.7 %collective-permute-done.5.refs_5_ = f32[4,4,32,128]{3,2,1,0:T(8,128)S(1)} collective-permute-done((f32[4,4,32,128]{3,2,1,0:T(8,128)S(1)}, f32[4,4,32,128]{3,2,1,0:T(8,128)S(1)}, u32[]{:S(2)}, u32[]{:S(2)}) %collective-permute-start.5) | collective-permute-done | bytes 262176 | tf_op jit(solution)/shard_map/ppermute | solution.py:316
  58.1 4.1 %window.1 = f32[8,32,128]{2,1,0:T(8,128)S(1)} custom-call(s32[1,1]{1,0:T(1,128)S(6)} %copy.11.source_ref, f32[4,4,32,128]{3,2,1,0:T(8,128)S(1)} %pad_maximum_fusion.mine_ref, f32[4,4,32,128]{3,2,1,0:T(8,128)S(1)} %collective-permute-done.refs_0_, f32[4,4,32,128]{3,2,1,0:T(8,128)S(1)} %collective-permute-done.1.refs_1_, ...), custom_call_target="tpu_custom_call" | custom-call | tf_op jit(solution)/shard_map/window/pallas_call | solution.py:337
  62.2 20.9 %all_to_all.15 = f32[32,8,128]{2,1,0:T(8,128)S(1)} all-to-all(f32[32,8,128]{2,1,0:T(8,128)S(1)} %bitcast.7), channel_id=1, replica_groups=mesh['shot'=32,'slab'=32] {'shot'}, dimensions={0} | all-to-all | bytes 262144 | tf_op jit(solution)/shard_map/all_to_all | solution.py:358
  83.1 14.1 %all_to_all.16 = f32[32,8,128]{2,1,0:T(8,128)S(1)} all-to-all(f32[32,8,128]{2,1,0:T(8,128)S(1)} %broadcast_in_dim.3), channel_id=1, replica_groups=mesh['shot'=32,'slab'=32] {'shot'}, dimensions={0} | all-to-all | bytes 262144 | tf_op jit(solution)/shard_map/all_to_all | solution.py:360
  97.2 0.7 fusion
  (2 shorter events, 0.0 us)
Async XLA Ops:
  1.6 37.4 %collective-permute-start = (f32[4,4,32,128]{3,2,1,0:T(8,128)S(1)}, f32[4,4,32,128]{3,2,1,0:T(8,128)S(1)}, u32[]{:S(2)}, u32[]{:S(2)}) collective-permute-start(f32[4,4,32,128]{3,2,1,0:T(8,128)S(1)} %pad_maximum_fusion.mine_ref), channel_id=1, source_target_pairs={{0,1},{1,2},{2,3},{3,4},{4,5},{5,6},{6,7},{7,8},{8,9},{9,10},{10,1... | collective-permute-start | bytes 786440 | tf_op jit(solution)/shard_map/ppermute | solution.py:316
  7.7 33.5 %all-to-all-start = ((f32[32,8,128]{2,1,0:T(8,128)}), f32[32,8,128]{2,1,0:T(8,128)S(1)}, u32[]{:S(2)}, u32[]{:S(2)}) async-start(f32[32,8,128]{2,1,0:T(8,128)} %route.1), calls=%async_computation | async-start | bytes 262144 | tf_op jit(solution)/shard_map/all_to_all | solution.py:322
  26.6 17.7 %collective-permute-start.1 = (f32[4,4,32,128]{3,2,1,0:T(8,128)S(1)}, f32[4,4,32,128]{3,2,1,0:T(8,128)S(1)}, u32[]{:S(2)}, u32[]{:S(2)}) collective-permute-start(f32[4,4,32,128]{3,2,1,0:T(8,128)S(1)} %pad_maximum_fusion.mine_ref), channel_id=1, source_target_pairs={{1,0},{2,1},{3,2},{4,3},{5,4},{6,5},{7,6},{8,7},{9,8},{10,9},{11,1... | collective-permute-start | bytes 786440 | tf_op jit(solution)/shard_map/ppermute | solution.py:316
  28.8 15.6 %collective-permute-start.2 = (f32[4,4,32,128]{3,2,1,0:T(8,128)S(1)}, f32[4,4,32,128]{3,2,1,0:T(8,128)S(1)}, u32[]{:S(2)}, u32[]{:S(2)}) collective-permute-start(f32[4,4,32,128]{3,2,1,0:T(8,128)S(1)} %pad_maximum_fusion.mine_ref), channel_id=1, source_target_pairs={{0,2},{1,3},{2,4},{3,5},{4,6},{5,7},{6,8},{7,9},{8,10},{9,11},{10,... | collective-permute-start | bytes 786440 | tf_op jit(solution)/shard_map/ppermute | solution.py:316
  31.9 12.4 %collective-permute-start.3 = (f32[4,4,32,128]{3,2,1,0:T(8,128)S(1)}, f32[4,4,32,128]{3,2,1,0:T(8,128)S(1)}, u32[]{:S(2)}, u32[]{:S(2)}) collective-permute-start(f32[4,4,32,128]{3,2,1,0:T(8,128)S(1)} %pad_maximum_fusion.mine_ref), channel_id=1, source_target_pairs={{2,0},{3,1},{4,2},{5,3},{6,4},{7,5},{8,6},{9,7},{10,8},{11,9},{12,... | collective-permute-start | bytes 786440 | tf_op jit(solution)/shard_map/ppermute | solution.py:316
  33.2 11.2 %collective-permute-start.4 = (f32[4,4,32,128]{3,2,1,0:T(8,128)S(1)}, f32[4,4,32,128]{3,2,1,0:T(8,128)S(1)}, u32[]{:S(2)}, u32[]{:S(2)}) collective-permute-start(f32[4,4,32,128]{3,2,1,0:T(8,128)S(1)} %pad_maximum_fusion.mine_ref), channel_id=1, source_target_pairs={{0,3},{1,4},{2,5},{3,6},{4,7},{5,8},{6,9},{7,10},{8,11},{9,12},{10... | collective-permute-start | bytes 786440 | tf_op jit(solution)/shard_map/ppermute | solution.py:316
  39.0 19.1 %collective-permute-start.5 = (f32[4,4,32,128]{3,2,1,0:T(8,128)S(1)}, f32[4,4,32,128]{3,2,1,0:T(8,128)S(1)}, u32[]{:S(2)}, u32[]{:S(2)}) collective-permute-start(f32[4,4,32,128]{3,2,1,0:T(8,128)S(1)} %pad_maximum_fusion.mine_ref), channel_id=1, source_target_pairs={{3,0},{4,1},{5,2},{6,3},{7,4},{8,5},{9,6},{10,7},{11,8},{12,9},{13... | collective-permute-start | bytes 786440 | tf_op jit(solution)/shard_map/ppermute | solution.py:316
  41.2 0.7 copy-start
where the time goes:
time: 98.4 us; the launch traced here: 97.9 us
  starting transfers between devices  36.6 us (37%)
  blocking collectives  34.9 us (35%)
  waiting for transfers between devices  13.9 us (14%)
  Pallas kernels  8.74 us (9%)
  between operations  1.39 us (1%)
  local copies, waits for them, and re-layouts  1.33 us (1%)
  other arithmetic  0.99 us (1%)
    all_to_all x1, blocking collectives, local(): lax.all_to_all(grads.reshape(SHOTS, 8, NY), 'shot', 0, 0, tiled=True)  20.9 us
    all_to_all x1, starting transfers between devices, local(): got = lax.all_to_all(send, 'slab', 0, 0, tiled=True)  18.9 us
    ppermute x6, starting transfers between devices, local(): near = [lax.ppermute(mine, 'slab', shift_pairs(shift)) for shift in SHIFTS]  17.6 us
    all_to_all x1, blocking collectives, local(): lax.all_to_all(total, 'shot', 0, 0, tiled=True).reshape(2, ROWS, NZ, NY)  14.1 us
    ppermute x6, waiting for transfers between devices, local(): near = [lax.ppermute(mine, 'slab', shift_pairs(shift)) for shift in SHIFTS]  13.8 us
    pallas_call x1, Pallas kernels, local(): pl.pallas_call(window_kernel, out_shape=jax.ShapeDtypeStruct((2 * ROWS, N...  4.09 us
    pallas_call x1, Pallas kernels, local(): pl.pallas_call(scatter_kernel, out_shape=(jax.ShapeDtypeStruct((BAND, NZ,...  2.53 us
    pallas_call x1, Pallas kernels, local(): pl.pallas_call(route_kernel, out_shape=jax.ShapeDtypeStruct((SLABS, 8, 12...  2.12 us
  transfers between devices with their start and end apart: 7, of which 2 were waited for; matrix products, arithmetic and copies ran while one was open for 0% of the time, Pallas kernels for 5%

commit v1 on v0

--- a/solution.py
+++ b/solution.py
@@ -19,7 +19,7 @@
 OWN = ROWS * REACH
 LO = 4
 BAND = 20
-SHIFTS = (1, -1, 2, -2, 3, -3)
+SHIFTS = (3, -3, 1, -1, 2, -2)
 
 NT = (((1,), (1,)), ((), ()))
 
@@ -53,8 +53,8 @@
     cells = (cell_ref[...] + 1).astype(jnp.float32)
     values = [obs_ref[n] for n in range(STEPS)] + [cells]
     total = None
-    splits = [split_bf16(v, 3) for v in values]
-    for p in range(3):
+    splits = [split_bf16(v, 2) for v in values]
+    for p in range(2):
         rows = [jnp.where(at_slot, s[p].astype(jnp.float32), 0.0) for s in splits]
         rows.append(jnp.zeros((CAP, rec), jnp.float32))
         block = jnp.concatenate(rows, axis=0).astype(jnp.bfloat16)

time: 98.4 us -> 98.1 us (level)
  the two profiles are of different devices: /device:TPU:3 before, /device:TPU:65 now
where the time goes in v1:
time: 98.1 us; the launch traced here: 97.6 us
  starting transfers between devices  37.2 us (38%)
  blocking collectives  35.1 us (36%)
  waiting for transfers between devices  12.9 us (13%)
  Pallas kernels  8.71 us (9%)
  between operations  1.39 us (1%)
  local copies, waits for them, and re-layouts  1.32 us (1%)
  other arithmetic  0.99 us (1%)
    all_to_all x1, blocking collectives, local(): lax.all_to_all(grads.reshape(SHOTS, 8, NY), 'shot', 0, 0, tiled=True)  21 us
    ppermute x6, starting transfers between devices, local(): near = [lax.ppermute(mine, 'slab', shift_pairs(shift)) for shift in SHIFTS]  19.2 us
    all_to_all x1, starting transfers between devices, local(): got = lax.all_to_all(send, 'slab', 0, 0, tiled=True)  18 us
    all_to_all x1, blocking collectives, local(): lax.all_to_all(total, 'shot', 0, 0, tiled=True).reshape(2, ROWS, NZ, NY)  14.1 us
    ppermute x6, waiting for transfers between devices, local(): near = [lax.ppermute(mine, 'slab', shift_pairs(shift)) for shift in SHIFTS]  12.9 us
    pallas_call x1, Pallas kernels, local(): pl.pallas_call(window_kernel, out_shape=jax.ShapeDtypeStruct((2 * ROWS, N...  4.08 us
    pallas_call x1, Pallas kernels, local(): pl.pallas_call(scatter_kernel, out_shape=(jax.ShapeDtypeStruct((BAND, NZ,...  2.53 us
    pallas_call x1, Pallas kernels, local(): pl.pallas_call(route_kernel, out_shape=jax.ShapeDtypeStruct((SLABS, 8, 12...  2.11 us
  transfers between devices with their start and end apart: 7, of which 2 were waited for; matrix products, arithmetic and copies ran while one was open for 0% of the time, Pallas kernels for 5%

profile of v1, /device:TPU:65, one launch (start us, length us, event | category | flops | bytes accessed | tf_op | source)
XLA Modules:
  0.0 97.6 jit_solution(2206771886305782257)
XLA Ops:
  0.6 1.0 pad_maximum_fusion.mine_ref
  1.6 4.9 %collective-permute-start = (f32[4,4,32,128]{3,2,1,0:T(8,128)S(1)}, f32[4,4,32,128]{3,2,1,0:T(8,128)S(1)}, u32[]{:S(2)}, u32[]{:S(2)}) collective-permute-start(f32[4,4,32,128]{3,2,1,0:T(8,128)S(1)} %pad_maximum_fusion.mine_ref), channel_id=1, source_target_pairs={{0,3},{1,4},{2,5},{3,6},{4,7},{5,8},{6,9},{7,10},{8,11},{9,12},{10... | collective-permute-start | bytes 786440 | tf_op jit(solution)/shard_map/ppermute | solution.py:316
  6.5 2.1 %route.1 = f32[32,8,128]{2,1,0:T(8,128)} custom-call(s32[1,512]{1,0:T(1,128)} %bitcast.13, s32[1,512]{1,0:T(1,128)} %cell_ref.1, f32[6,1,512]{2,1,0:T(1,128)} %bitcast.12), custom_call_target="tpu_custom_call" | custom-call | tf_op jit(solution)/shard_map/route/pallas_call | solution.py:317
  8.6 18.0 %all-to-all-start = ((f32[32,8,128]{2,1,0:T(8,128)}), f32[32,8,128]{2,1,0:T(8,128)S(1)}, u32[]{:S(2)}, u32[]{:S(2)}) async-start(f32[32,8,128]{2,1,0:T(8,128)} %route.1), calls=%async_computation | async-start | bytes 262144 | tf_op jit(solution)/shard_map/all_to_all | solution.py:322
  26.6 1.3 %collective-permute-start.1 = (f32[4,4,32,128]{3,2,1,0:T(8,128)S(1)}, f32[4,4,32,128]{3,2,1,0:T(8,128)S(1)}, u32[]{:S(2)}, u32[]{:S(2)}) collective-permute-start(f32[4,4,32,128]{3,2,1,0:T(8,128)S(1)} %pad_maximum_fusion.mine_ref), channel_id=1, source_target_pairs={{3,0},{4,1},{5,2},{6,3},{7,4},{8,5},{9,6},{10,7},{11,8},{12,9},{13... | collective-permute-start | bytes 786440 | tf_op jit(solution)/shard_map/ppermute | solution.py:316
  27.9 3.9 %collective-permute-start.2 = (f32[4,4,32,128]{3,2,1,0:T(8,128)S(1)}, f32[4,4,32,128]{3,2,1,0:T(8,128)S(1)}, u32[]{:S(2)}, u32[]{:S(2)}) collective-permute-start(f32[4,4,32,128]{3,2,1,0:T(8,128)S(1)} %pad_maximum_fusion.mine_ref), channel_id=1, source_target_pairs={{0,1},{1,2},{2,3},{3,4},{4,5},{5,6},{6,7},{7,8},{8,9},{9,10},{10,1... | collective-permute-start | bytes 786440 | tf_op jit(solution)/shard_map/ppermute | solution.py:316
  31.9 2.2 %collective-permute-start.3 = (f32[4,4,32,128]{3,2,1,0:T(8,128)S(1)}, f32[4,4,32,128]{3,2,1,0:T(8,128)S(1)}, u32[]{:S(2)}, u32[]{:S(2)}) collective-permute-start(f32[4,4,32,128]{3,2,1,0:T(8,128)S(1)} %pad_maximum_fusion.mine_ref), channel_id=1, source_target_pairs={{1,0},{2,1},{3,2},{4,3},{5,4},{6,5},{7,6},{8,7},{9,8},{10,9},{11,1... | collective-permute-start | bytes 786440 | tf_op jit(solution)/shard_map/ppermute | solution.py:316
  34.1 4.9 %collective-permute-start.4 = (f32[4,4,32,128]{3,2,1,0:T(8,128)S(1)}, f32[4,4,32,128]{3,2,1,0:T(8,128)S(1)}, u32[]{:S(2)}, u32[]{:S(2)}) collective-permute-start(f32[4,4,32,128]{3,2,1,0:T(8,128)S(1)} %pad_maximum_fusion.mine_ref), channel_id=1, source_target_pairs={{0,2},{1,3},{2,4},{3,5},{4,6},{5,7},{6,8},{7,9},{8,10},{9,11},{10,... | collective-permute-start | bytes 786440 | tf_op jit(solution)/shard_map/ppermute | solution.py:316
  39.0 0.0 collective-permute-done.refs_0_
  39.0 1.9 %collective-permute-start.5 = (f32[4,4,32,128]{3,2,1,0:T(8,128)S(1)}, f32[4,4,32,128]{3,2,1,0:T(8,128)S(1)}, u32[]{:S(2)}, u32[]{:S(2)}) collective-permute-start(f32[4,4,32,128]{3,2,1,0:T(8,128)S(1)} %pad_maximum_fusion.mine_ref), channel_id=1, source_target_pairs={{2,0},{3,1},{4,2},{5,3},{6,4},{7,5},{8,6},{9,7},{10,8},{11,9},{12,... | collective-permute-start | bytes 786440 | tf_op jit(solution)/shard_map/ppermute | solution.py:316
  41.6 0.0 all-to-all-done.got_ref
  41.6 0.0 copy-start
  41.6 0.6 copy-done
  42.3 2.5 %scatter.1 = (f32[20,32,128]{2,1,0:T(8,128)S(1)}, f32[6,20,32,128]{3,2,1,0:T(8,128)S(1)}, f32[8,128]{1,0:T(8,128)S(1)}) custom-call(f32[1,6]{1,0:T(1,128)S(1)} %copy-done, f32[32,8,128]{2,1,0:T(8,128)S(1)} %all-to-all-done.got_ref), custom_call_target="tpu_custom_call" | custom-call | tf_op jit(solution)/shard_map/scatter/pallas_call | solution.py:325
  44.8 0.0 collective-permute-done.1.refs_1_
  44.8 0.0 collective-permute-done.2.refs_2_
  44.8 6.1 %collective-permute-done.3.refs_3_ = f32[4,4,32,128]{3,2,1,0:T(8,128)S(1)} collective-permute-done((f32[4,4,32,128]{3,2,1,0:T(8,128)S(1)}, f32[4,4,32,128]{3,2,1,0:T(8,128)S(1)}, u32[]{:S(2)}, u32[]{:S(2)}) %collective-permute-start.3) | collective-permute-done | bytes 262176 | tf_op jit(solution)/shard_map/ppermute | solution.py:316
  50.9 0.0 collective-permute-done.4.refs_4_
  50.9 6.8 %collective-permute-done.5.refs_5_ = f32[4,4,32,128]{3,2,1,0:T(8,128)S(1)} collective-permute-done((f32[4,4,32,128]{3,2,1,0:T(8,128)S(1)}, f32[4,4,32,128]{3,2,1,0:T(8,128)S(1)}, u32[]{:S(2)}, u32[]{:S(2)}) %collective-permute-start.5) | collective-permute-done | bytes 262176 | tf_op jit(solution)/shard_map/ppermute | solution.py:316
  57.7 4.1 %window.1 = f32[8,32,128]{2,1,0:T(8,128)S(1)} custom-call(s32[1,1]{1,0:T(1,128)S(6)} %copy.11.source_ref, f32[4,4,32,128]{3,2,1,0:T(8,128)S(1)} %pad_maximum_fusion.mine_ref, f32[4,4,32,128]{3,2,1,0:T(8,128)S(1)} %collective-permute-done.refs_0_, f32[4,4,32,128]{3,2,1,0:T(8,128)S(1)} %collective-permute-done.1.refs_1_, ...), custom_call_target="tpu_custom_call" | custom-call | tf_op jit(solution)/shard_map/window/pallas_call | solution.py:337
  61.8 21.0 %all_to_all.15 = f32[32,8,128]{2,1,0:T(8,128)S(1)} all-to-all(f32[32,8,128]{2,1,0:T(8,128)S(1)} %bitcast.7), channel_id=1, replica_groups=mesh['shot'=32,'slab'=32] {'shot'}, dimensions={0} | all-to-all | bytes 262144 | tf_op jit(solution)/shard_map/all_to_all | solution.py:358
  82.9 14.1 %all_to_all.16 = f32[32,8,128]{2,1,0:T(8,128)S(1)} all-to-all(f32[32,8,128]{2,1,0:T(8,128)S(1)} %broadcast_in_dim.3), channel_id=1, replica_groups=mesh['shot'=32,'slab'=32] {'shot'}, dimensions={0} | all-to-all | bytes 262144 | tf_op jit(solution)/shard_map/all_to_all | solution.py:360
  96.9 0.7 fusion
  (2 shorter events, 0.0 us)
Async XLA Ops:
  1.6 37.4 %collective-permute-start = (f32[4,4,32,128]{3,2,1,0:T(8,128)S(1)}, f32[4,4,32,128]{3,2,1,0:T(8,128)S(1)}, u32[]{:S(2)}, u32[]{:S(2)}) collective-permute-start(f32[4,4,32,128]{3,2,1,0:T(8,128)S(1)} %pad_maximum_fusion.mine_ref), channel_id=1, source_target_pairs={{0,3},{1,4},{2,5},{3,6},{4,7},{5,8},{6,9},{7,10},{8,11},{9,12},{10... | collective-permute-start | bytes 786440 | tf_op jit(solution)/shard_map/ppermute | solution.py:316
  8.6 33.0 %all-to-all-start = ((f32[32,8,128]{2,1,0:T(8,128)}), f32[32,8,128]{2,1,0:T(8,128)S(1)}, u32[]{:S(2)}, u32[]{:S(2)}) async-start(f32[32,8,128]{2,1,0:T(8,128)} %route.1), calls=%async_computation | async-start | bytes 262144 | tf_op jit(solution)/shard_map/all_to_all | solution.py:322
  26.6 18.2 %collective-permute-start.1 = (f32[4,4,32,128]{3,2,1,0:T(8,128)S(1)}, f32[4,4,32,128]{3,2,1,0:T(8,128)S(1)}, u32[]{:S(2)}, u32[]{:S(2)}) collective-permute-start(f32[4,4,32,128]{3,2,1,0:T(8,128)S(1)} %pad_maximum_fusion.mine_ref), channel_id=1, source_target_pairs={{3,0},{4,1},{5,2},{6,3},{7,4},{8,5},{9,6},{10,7},{11,8},{12,9},{13... | collective-permute-start | bytes 786440 | tf_op jit(solution)/shard_map/ppermute | solution.py:316
  27.9 16.9 %collective-permute-start.2 = (f32[4,4,32,128]{3,2,1,0:T(8,128)S(1)}, f32[4,4,32,128]{3,2,1,0:T(8,128)S(1)}, u32[]{:S(2)}, u32[]{:S(2)}) collective-permute-start(f32[4,4,32,128]{3,2,1,0:T(8,128)S(1)} %pad_maximum_fusion.mine_ref), channel_id=1, source_target_pairs={{0,1},{1,2},{2,3},{3,4},{4,5},{5,6},{6,7},{7,8},{8,9},{9,10},{10,1... | collective-permute-start | bytes 786440 | tf_op jit(solution)/shard_map/ppermute | solution.py:316
  31.9 19.1 %collective-permute-start.3 = (f32[4,4,32,128]{3,2,1,0:T(8,128)S(1)}, f32[4,4,32,128]{3,2,1,0:T(8,128)S(1)}, u32[]{:S(2)}, u32[]{:S(2)}) collective-permute-start(f32[4,4,32,128]{3,2,1,0:T(8,128)S(1)} %pad_maximum_fusion.mine_ref), channel_id=1, source_target_pairs={{1,0},{2,1},{3,2},{4,3},{5,4},{6,5},{7,6},{8,7},{9,8},{10,9},{11,1... | collective-permute-start | bytes 786440 | tf_op jit(solution)/shard_map/ppermute | solution.py:316
  34.1 16.8 %collective-permute-start.4 = (f32[4,4,32,128]{3,2,1,0:T(8,128)S(1)}, f32[4,4,32,128]{3,2,1,0:T(8,128)S(1)}, u32[]{:S(2)}, u32[]{:S(2)}) collective-permute-start(f32[4,4,32,128]{3,2,1,0:T(8,128)S(1)} %pad_maximum_fusion.mine_ref), channel_id=1, source_target_pairs={{0,2},{1,3},{2,4},{3,5},{4,6},{5,7},{6,8},{7,9},{8,10},{9,11},{10,... | collective-permute-start | bytes 786440 | tf_op jit(solution)/shard_map/ppermute | solution.py:316
  39.0 18.7 %collective-permute-start.5 = (f32[4,4,32,128]{3,2,1,0:T(8,128)S(1)}, f32[4,4,32,128]{3,2,1,0:T(8,128)S(1)}, u32[]{:S(2)}, u32[]{:S(2)}) collective-permute-start(f32[4,4,32,128]{3,2,1,0:T(8,128)S(1)} %pad_maximum_fusion.mine_ref), channel_id=1, source_target_pairs={{2,0},{3,1},{4,2},{5,3},{6,4},{7,5},{8,6},{9,7},{10,8},{11,9},{12,... | collective-permute-start | bytes 786440 | tf_op jit(solution)/shard_map/ppermute | solution.py:316
  41.6 0.7 copy-start
